TPU v7x, 128 devices: a whole 4x4x4 slice. The times are simulated.
128 devices in a mesh: row: 16 (over y_hi, x, core), col: 8 (over z, y_lo).
Axes of the slice: x: 4, y: 4 (y_hi: 2, y_lo: 2; y = y_hi * 2 + y_lo), z: 4, core: 2. Of those that a mesh axis runs over, the one named last changes fastest.
Arguments:
- unsieved_electron_density: bfloat16 [8192, 8192], P('row', 'col')
- present_patch_indicator: int32 [64, 64], P('row', 'col'), may hold values 0 or 1
- surviving_patch_indicator: int32 [64, 64], P('row', 'col'), may hold values 0 or 1
- proprietor_rows: int32 [64, 64], P('row', 'col'), may hold values from 0 to 15, as said below
Outputs:
- delivered: bfloat16 [1024, 8, 16384], P('row', 'col')
Inputs may be any that keep to these rules, and one draw needn't show every extreme that they name: `proprietor_rows`: the 4 x 8 blocks held by one device include at most 4 with the same owner. In each block-column group some owner receives 4 blocks from every device of the group.
All inputs are finite; a program needn't handle non-finite values. No bound on the sum of `present_patch_indicator` or of `surviving_patch_indicator` on one device may be relied on, other than what follows from the above.
Results may differ from a plain program's by a relative error of at most 0.0049.
Values may be sent and summed in bfloat16 or wider, within the bound.
A program may use at most 128 MiB of HBM per device.

v0:
```python
import jax
import jax.numpy as jnp
from jax import lax
from jax.sharding import PartitionSpec as P


def inflated_tile_flags(sieve_pattern, tile_span):
    return jnp.repeat(jnp.repeat(sieve_pattern, tile_span, 0), tile_span, 1)


def per_device(
    unsieved_electron_density, present_patch_indicator, surviving_patch_indicator, proprietor_rows
):
    tile_span = unsieved_electron_density.shape[0] // present_patch_indicator.shape[0]
    group_size = lax.axis_size("row")
    sieved_electron_density = unsieved_electron_density * inflated_tile_flags(
        present_patch_indicator, tile_span
    ).astype(jnp.bfloat16)
    retained_tile_flags = inflated_tile_flags(surviving_patch_indicator, tile_span).astype(
        jnp.float32
    )
    gathered = lax.all_gather(sieved_electron_density, "row", axis=0, tiled=True)

    def multiply(left_tile):
        return jnp.dot(
            lax.all_gather(left_tile, "col", axis=1, tiled=True),
            gathered,
            preferred_element_type=jnp.float32,
        )

    thinned_self_multiply = multiply(sieved_electron_density) * retained_tile_flags
    squared = thinned_self_multiply.astype(jnp.bfloat16)
    cubed = multiply(squared)
    purified = (3.0 * thinned_self_multiply - 2.0 * cubed).astype(jnp.bfloat16)
    block_rows, block_cols = present_patch_indicator.shape
    block_count = block_rows * block_cols
    slot_count = 2 * block_count // group_size
    blocks = purified.reshape(block_rows, tile_span, block_cols, tile_span).transpose(0, 2, 1, 3)
    blocks = blocks.reshape(block_count, tile_span * tile_span)
    owner_list = proprietor_rows.reshape(-1)
    position = jnp.arange(block_count, dtype=jnp.int32)
    same_owner = owner_list[:, None] == owner_list[None, :]
    earlier = position[None, :] < position[:, None]
    slot = jnp.sum((same_owner & earlier).astype(jnp.int32), axis=1)
    target = owner_list * slot_count + slot
    outgoing = jnp.zeros((group_size * slot_count, tile_span * tile_span), jnp.bfloat16)
    outgoing = outgoing.at[target].set(blocks)
    arrived = lax.all_to_all(outgoing, "row", split_axis=0, concat_axis=0, tiled=True)
    return arrived.reshape(group_size * slot_count, 1, tile_span * tile_span)


def solution(mesh):
    placed = (P("row", "col"), P("row", "col"), P("row", "col"), P("row", "col"))
    return jax.shard_map(
        per_device, mesh=mesh, in_specs=placed, out_specs=P("row", "col", None), check_vma=False
    )
```

profile of v0, /device:TPU:1, one launch (start us, length us, event | category | flops | bytes accessed | tf_op | source)
XLA Modules:
  0.0 542.2 jit_solution(2517529669480747505)
XLA Ops:
  6.5 0.0 all-gather.4.cloned.1.call-start
  6.5 0.7 convert_element_type.32
  7.2 0.6 broadcast_in_dim.20
  7.9 0.0 copy-start.1
  7.9 2.3 bitcast_multiply_fusion.1
  10.2 0.0 all-gather.4.cloned.1.call-update
  10.2 0.0 all-gather.6.cloned.1.call-start
  10.3 0.7 all-gather.6.cloned.1.call-update
  11.0 0.0 all-gather.8.cloned.1.call-start
  11.0 0.0 copy-done.1
  11.1 170.9 %all-gather.4.cloned.1.call-done = bf16[512,8192]{1,0:T(8,128)(2,1)} async-done(((bf16[512,1024]{1,0:T(8,128)(2,1)}), bf16[512,8192]{1,0:T(8,128)(2,1)}) %all-gather.4.cloned.1.call-update) | async-done | bytes 8388624 | tf_op jit(solution)/shard_map/all_gather | solution.py:26
  181.9 114.2 %all-gather.6.cloned.1.call-done = bf16[8192,1024]{1,0:T(8,128)(2,1)} async-done(((bf16[512,1024]{1,0:T(8,128)(2,1)}), bf16[8192,1024]{1,0:T(8,128)(2,1)}) %all-gather.6.cloned.1.call-update) | async-done | bytes 16777232 | tf_op jit(solution)/shard_map/all_gather | solution.py:22
  296.1 0.6 broadcast_in_dim.22
  296.7 0.0 copy-start
  296.7 15.8 %fusion.5 = (bf16[512,1024]{1,0:T(8,128)(2,1)}, f32[512,1024]{1,0:T(8,128)S(1)}) fusion(f32[64,8,8,128]{3,2,1,0:T(8,128)S(1)} %bitcast.33, bf16[512,8192]{1,0:T(8,128)(2,1)} %all-gather.4.cloned.1.call-done, bf16[8192,1024]{1,0:T(8,128)(2,1)} %all-gather.6.cloned.1.call-done), kind=kOutput, calls=%fused_computation.15 | convolution fusion | flops 8590983168 | bytes 30408704 | tf_op jit(solution)/shard_map/dot_general | solution.py:25
  312.5 0.0 all-gather.8.cloned.1.call-update
  312.5 0.0 copy-done
  312.6 0.1 eq.15
  312.6 0.1 mul.36
  312.7 0.2 convert_reduce_fusion
  312.9 165.5 %all-gather.8.cloned.1.call-done = bf16[512,8192]{1,0:T(8,128)(2,1)} async-done(((bf16[512,1024]{1,0:T(8,128)(2,1)}), bf16[512,8192]{1,0:T(8,128)(2,1)}) %all-gather.8.cloned.1.call-update) | async-done | bytes 8388624 | tf_op jit(solution)/shard_map/all_gather | solution.py:26
  478.4 14.8 %fusion = bf16[64,8,8,128]{3,1,2,0:T(8,128)(2,1)S(1)} fusion(bf16[512,8192]{1,0:T(8,128)(2,1)} %all-gather.8.cloned.1.call-done, bf16[8192,1024]{1,0:T(8,128)(2,1)} %all-gather.6.cloned.1.call-done, f32[512,1024]{1,0:T(8,128)S(1)} %get-tuple-element.6), kind=kOutput, calls=%fused_computation.3 | convolution fusion | flops 8592031744 | bytes 28311552 | tf_op jit(solution)/shard_map/dot_general | solution.py:25
  493.2 0.3 copy.7
  493.4 2.7 scatter_custom_fusion
  496.1 2.2 all_to_all.6
  498.3 35.3 %all_to_all.9 = bf16[16,4,16384]{2,1,0:T(4,128)(2,1)S(1)} all-to-all(bf16[16,4,16384]{2,1,0:T(4,128)(2,1)} %all_to_all.6), channel_id=1, replica_groups=mesh['row'=16,'col'=8] {'row'}, dimensions={0} | all-to-all | bytes 4194304 | tf_op jit(solution)/shard_map/all_to_all | solution.py:48
  533.7 2.0 reshape.53
  (5 shorter events, 0.1 us)
Async XLA Ops:
  6.5 175.4 %all-gather.4.cloned.1.call-start = ((), (), s32[]{:S(2)}) async-start(), calls=%async_computation.1 | async-start | bytes 9437184 | tf_op jit(solution)/shard_map/all_gather | solution.py:26
  7.9 3.2 copy-start.1
  10.2 285.8 %all-gather.6.cloned.1.call-start = ((), (), s32[]{:S(2)}) async-start(), calls=%async_computation.2 | async-start | bytes 17825792 | tf_op jit(solution)/shard_map/all_gather | solution.py:22
  11.0 467.4 %all-gather.8.cloned.1.call-start = ((), (), s32[]{:S(2)}) async-start(), calls=%async_computation.3 | async-start | bytes 9437184 | tf_op jit(solution)/shard_map/all_gather | solution.py:26
  296.7 15.9 %copy-start = (s32[4,8]{1,0:T(4,128)S(1)}, s32[4,8]{1,0:T(4,128)}, u32[]{:S(2)}) copy-start(s32[4,8]{1,0:T(4,128)} %param.7) | copy-start | bytes 388
Sparse Core Ops, SparseCore 0:
  10.4 171.5 all-gather.3
  184.4 111.6 all-gather.5
  312.7 165.6 all-gather.7
where the time goes:
time: 542 us
  waiting for transfers between devices  451 us (83%)
  blocking collectives  35.3 us (7%)
  matrix products  30.6 us (6%)
  between operations  13.2 us (2%)
  local copies, waits for them, and re-layouts  8.57 us (2%)
    all_gather x2, waiting for transfers between devices, multiply(): lax.all_gather(left_tile, 'col', axis=1, tiled=True)  336 us
    all_gather x1, waiting for transfers between devices, per_device(): lax.all_gather(sieved_electron_density, 'row', axis=0, tiled=True)  114 us
    all_to_all x1, blocking collectives, per_device(): lax.all_to_all(outgoing, 'row', split_axis=0, concat_axis=0, tiled=True)  35.3 us
    dot_general x2, matrix products, multiply(): jnp.dot(lax.all_gather(left_tile, 'col', axis=1, tiled=True), gathered, p...  30.6 us
  transfers between devices with their start and end apart: 3, of which 3 were waited for; matrix products, arithmetic and copies ran while one was open for 0% of the time, Pallas kernels for 0%

commit v1 on v0

v1 whole, which is shorter than its diff:
```python
import functools

import jax
import jax.numpy as jnp
from jax import lax
from jax.experimental import pallas as pl
from jax.experimental.pallas import tpu as pltpu
from jax.sharding import PartitionSpec as P

MESH = pl.DeviceIdType.MESH
B = 128
ROWS = 512
COLS = 1024
NCH = 4
W = COLS // NCH
SUB = ROWS // W
HS = SUB // 2
BW = W // B
F32 = jnp.float32
BF16 = jnp.bfloat16


def coords():
    r = lax.axis_index("row")
    c = lax.axis_index("col")
    return (r // 2) % 4, (r // 8) * 2 + c % 2, c // 2, r % 2


def dev(x, y, z, core):
    x = (x + 8) % 4
    y = (y + 8) % 4
    z = (z + 8) % 4
    return ((y // 2) * 8 + x * 2 + core, z * 2 + y % 2)


def cols(at, width=W):
    return pl.ds(pl.multiple_of(at * W, W), width)


def step_kernel(
    u, present, surviving, out,
    own, right, left, fleft, fown, sums, ssend, srecv, csend, crecv, total,
    s1s, s1r, s2s, s2r, s3s, s3r, ds_, dr, loc, ls, lr, lrs, lrr, fs, fr, frs, frr, xs, xr, cs, cr,
):
    x, y, z, core = coords()
    yl = y % 2
    q = (x + y) % 2
    here = (x, y, z, core)
    bar = pltpu.get_barrier_semaphore()
    near = [
        dev(x + 1, y, z, core), dev(x - 1, y, z, core), dev(x, y + 1, z, core), dev(x, y - 1, z, core),
        dev(x, y + 2, z, core), dev(x, y, z + 1, core), dev(x, y, z - 1, core), dev(x, y, z, 1 - core),
    ]
    xp, xm, yp, ym, yy, zp, zm, other = near
    partner = dev(x, (y // 2) * 2 + 1 - yl, z, core)
    for d in near:
        pl.semaphore_signal(bar, inc=1, device_id=d, device_id_type=MESH)

    def rc(src, dst, ssem, rsem, to):
        return pltpu.make_async_remote_copy(
            src_ref=src, dst_ref=dst, send_sem=ssem, recv_sem=rsem, device_id=to, device_id_type=MESH
        )

    pending = []

    def go(copy):
        copy.start()
        pending.append(copy)

    def piece(j, xs_, ys_, h):
        xs_ = (xs_ + 8) % 4
        ys_ = (ys_ + 8) % 4
        slab = (ys_ // 2) * 2 + xs_ // 2
        k = core * (NCH // 2) + h * HS
        return right.at[j, pl.ds(k, HS), slab, :, cols(ys_ % 2)]

    def sieve(j):
        for i in range(4):
            for b in range(BW):
                keep = present[i, j * BW + b] != 0
                block = u[i * B:(i + 1) * B, j * W + b * B:j * W + (b + 1) * B]
                r0 = (i * B) % W
                kept = jnp.where(keep, block, jnp.zeros_like(block))
                own[0, j, (i * B) // W, r0:r0 + B, b * B:(b + 1) * B] = kept

    def st1(j):
        for h in range(2):
            part = pl.ds(h * HS, HS)
            go(rc(own.at[0, j, part], own.at[1, j, part], s1s.at[j, h], s1r.at[j, h], xm if h else xp))

    def st1_wait(j):
        for h in range(2):
            part = pl.ds(h * HS, HS)
            rc(own.at[0, j, part], own.at[1, j, part], s1s.at[j, h], s1r.at[j, h], xp).wait_recv()

    def shift(h):
        return 1 if h else -1

    def st2(j):
        st1_wait(j)
        locals_ = []
        for h in range(2):
            part = pl.ds(h * HS, HS)
            wrong = own.at[1 - q, j, part]
            fine = own.at[q, j, part]
            wx = x + (1 - q) * shift(h)
            fx = x + q * shift(h)
            go(rc(wrong, piece(j, wx, y, h), s2s.at[j, h, 0], s2r.at[j, h, 0], yp))
            go(rc(wrong, piece(j, wx, y, h), s2s.at[j, h, 1], s2r.at[j, h, 1], ym))
            go(rc(fine, piece(j, fx, y, h), s2s.at[j, h, 2], s2r.at[j, h, 2], yy))
            c = pltpu.make_async_copy(fine, piece(j, fx, y, h), loc.at[j, h])
            c.start()
            locals_.append(c)
        return locals_

    def st3(j, locals_):
        for d, kind in ((0, None), (-1, 0), (1, 1), (2, 2)):
            for h in range(2):
                at = piece(j, x + q * shift(h), y + d, h)
                if kind is None:
                    locals_[h].wait()
                else:
                    rc(at, at, s2s.at[j, h, kind], s2r.at[j, h, kind], yp).wait_recv()
                n = d % 4
                to = dev(x + shift(h) * (1 - 2 * q), y, z, core)
                go(rc(at, at, s3s.at[j, n, h], s3r.at[j, n, h], to))
                rc(at, at, ds_.at[j], dr.at[j], other).start()

    def share(j):
        for d in (0, -1, 1, 2):
            for h in range(2):
                at = piece(j, x + q * shift(h) + 2, y + d, h)
                rc(at, at, s3s.at[j, d % 4, h], s3r.at[j, d % 4, h], xp).wait_recv()
                rc(at, at, ds_.at[j], dr.at[j], other).start()

    def half(j, c):
        return right.at[j, pl.ds(c * (NCH // 2), NCH // 2)]

    def ring_send(src, buf, j, ssem, rsem):
        go(rc(src, buf.at[j, :, :, cols(z)], ssem.at[j, 0], rsem.at[j, 0], zp))
        go(rc(src, buf.at[j, :, :, cols(z)], ssem.at[j, 1], rsem.at[j, 1], zm))

    def ring_relay(buf, j, ssem, rsem, rss, rsr):
        for k, (frm, to) in enumerate(((-1, zp), (1, zm))):
            at = buf.at[j, :, :, cols((z + frm + 4) % 4)]
            rc(at, at, ssem.at[j, k], rsem.at[j, k], to).wait_recv()
            on = buf.at[j, pl.ds(k * HS, HS), :, cols((z + frm + 4) % 4)]
            go(rc(on, on, rss.at[j, k], rsr.at[j, k], to))

    def ring_wait(buf, j, rss, rsr):
        for k in range(2):
            at = buf.at[j, pl.ds(k * HS, HS), :, cols((z + 2) % 4)]
            rc(at, at, rss.at[j, k], rsr.at[j, k], zp).wait_recv()

    def square(j):
        rc(half(j, core), half(j, 1 - core), ds_.at[j], dr.at[j], other).wait_recv()

        @pl.loop(0, SUB)
        def _(m):
            acc = None
            for k in range(NCH):
                d = jnp.dot(left[k, m], right[j, k].reshape(4 * W, 2 * W), preferred_element_type=F32)
                acc = d if acc is None else acc + d
            sums[m] = acc

        @pl.loop(0, SUB)
        def _(m):
            ssend[j, m] = sums[m, :, cols(1 - yl)].astype(BF16)

        go(rc(ssend.at[j], srecv.at[j], xs.at[j], xr.at[j], partner))

    def sift(j):
        rc(ssend.at[j], srecv.at[j], xs.at[j], xr.at[j], partner).wait_recv()
        for i in range(4):
            m, r0 = (i * B) // W, (i * B) % W
            for b in range(BW):
                keep = surviving[i, j * BW + b].astype(F32)
                mine = pl.ds(pl.multiple_of(yl * W + b * B, B), B)
                theirs = pl.ds(pl.multiple_of((1 - yl) * W + b * B, B), B)
                rows, cb = slice(r0, r0 + B), slice(b * B, (b + 1) * B)
                f = (sums[m, rows, mine] + srecv[j, m, rows, cb].astype(F32)) * keep
                fb = f.astype(BF16)
                fown[j, m, rows, cb] = fb
                fleft[j, m, rows, pl.ds(pl.multiple_of(z * W + b * B, B), B)] = fb
                total[j, m, rows, mine] = f * -1.5
                total[j, m, rows, theirs] = jnp.zeros((B, B), F32)
        ring_send(fown.at[j], fleft, j, fs, fr)

    def cube(ks, j):
        if not ks:
            return

        @pl.loop(0, SUB)
        def _(m):
            acc = total[j, m]
            for k in ks:
                acc += jnp.dot(fleft[k, m], right[j, k].reshape(4 * W, 2 * W), preferred_element_type=F32)
            total[j, m] = acc

    def cube_send(j):
        @pl.loop(0, SUB)
        def _(m):
            csend[j, m] = total[j, m, :, cols(1 - yl)].astype(BF16)

        go(rc(csend.at[j], crecv.at[j], cs.at[j], cr.at[j], partner))

    def finish(j):
        rc(csend.at[j], crecv.at[j], cs.at[j], cr.at[j], partner).wait_recv()
        for i in range(4):
            m, r0 = (i * B) // W, (i * B) % W
            for b in range(BW):
                mine = pl.ds(pl.multiple_of(yl * W + b * B, B), B)
                rows, cb = slice(r0, r0 + B), slice(b * B, (b + 1) * B)
                v = (total[j, m, rows, mine] + crecv[j, m, rows, cb].astype(F32)) * -2.0
                out[i * 8 + j * BW + b] = v.astype(BF16)

    own_lefts = []
    sieve(0)
    pl.semaphore_wait(bar, 8)
    st1(0)
    for j in range(NCH):
        if j:
            sieve(j)
        if j == 1:
            st1(1)
        own_left = pltpu.make_async_copy(own.at[0, j], left.at[j, :, :, cols(z)], lrs.at[j, 2])
        own_left.start()
        own_lefts.append(own_left)
        ring_send(own.at[0, j], left, j, ls, lr)

    held = {}
    fdone = 0
    done = {j: 0 for j in range(NCH)}
    left_relays = {0: [0], 1: list(range(1, NCH - 1)), 2: [NCH - 1]}
    for t in range(NCH + 2):
        if t < NCH:
            held[t] = st2(t)
            if t + 2 < NCH:
                st1(t + 2)
        if 0 <= t - 1 < NCH:
            st3(t - 1, held[t - 1])
        for j in left_relays.get(t, []):
            ring_relay(left, j, ls, lr, lrs, lrr)
        s = t - 2
        if 0 <= s:
            share(s)
            if s == 0:
                for j in range(NCH):
                    ring_wait(left, j, lrs, lrr)
                    own_lefts[j].wait()
            square(s)
            if s >= 1:
                ring_relay(fleft, s - 1, fs, fr, frs, frr)
            if s >= 2:
                ring_wait(fleft, s - 2, frs, frr)
                fdone = s - 1
            for j in range(s):
                cube(list(range(done[j], fdone)), j)
                done[j] = fdone
            sift(s)
    last = NCH - 1
    if NCH >= 2:
        ring_wait(fleft, last - 1, frs, frr)
        for j in range(NCH):
            cube(list(range(done[j], last)), j)
    ring_relay(fleft, last, fs, fr, frs, frr)
    ring_wait(fleft, last, frs, frr)
    for j in range(NCH):
        cube([last], j)
        cube_send(j)
    for j in range(NCH):
        rc(half(j, core), half(j, 1 - core), ds_.at[j], dr.at[j], other).wait_send()
    for c in pending[:-NCH]:
        c.wait_send()
    for j in range(NCH):
        finish(j)
    for c in pending[-NCH:]:
        c.wait_send()


def deliver_kernel(p, index, valid, out, packed, ss, rs, loc):
    r = lax.axis_index("row")
    c = lax.axis_index("col")
    n = 16
    bar = pltpu.get_barrier_semaphore()
    for d in range(1, n):
        pl.semaphore_signal(bar, inc=1, device_id=((r + d) % n, c), device_id_type=MESH)

    @pl.loop(0, 64)
    def _(s):
        block = p[index[s]]
        packed[s] = jnp.where(valid[s] != 0, block, jnp.zeros_like(block))

    pl.semaphore_wait(bar, n - 1)
    mine = pltpu.make_async_copy(packed.at[pl.ds(r * 4, 4)], out.at[pl.ds(r * 4, 4)], loc)
    mine.start()
    copies = []
    for d in range(1, n):
        to = (r + d) % n
        copy = pltpu.make_async_remote_copy(
            src_ref=packed.at[pl.ds(to * 4, 4)], dst_ref=out.at[pl.ds(r * 4, 4)],
            send_sem=ss.at[d], recv_sem=rs.at[d], device_id=(to, c), device_id_type=MESH,
        )
        copy.start()
        copies.append(copy)
    mine.wait()
    for copy in copies:
        copy.wait()


def slots(owners):
    flat = owners.reshape(-1)
    at = jnp.arange(32, dtype=jnp.int32)
    same = flat[:, None] == flat[None, :]
    slot = jnp.sum((same & (at[None, :] < at[:, None])).astype(jnp.int32), axis=1)
    target = flat * 4 + slot
    hit = target[None, :] == jnp.arange(64, dtype=jnp.int32)[:, None]
    return jnp.sum(jnp.where(hit, at[None, :], 0), axis=1), jnp.sum(hit.astype(jnp.int32), axis=1)


def per_device(u, present, surviving, owners):
    vm = pl.BlockSpec(memory_space=pltpu.VMEM)
    sm = pl.BlockSpec(memory_space=pltpu.SMEM)
    dma = pltpu.SemaphoreType.DMA
    vmem = pltpu.VMEM
    index, valid = slots(owners)
    purified = pl.pallas_call(
        step_kernel,
        out_shape=jax.ShapeDtypeStruct((32, B, B), BF16),
        in_specs=[vm, sm, sm],
        out_specs=vm,
        scratch_shapes=[
            vmem((2, NCH, SUB, W, W), BF16),
            vmem((NCH, NCH, 4, W, 2 * W), BF16),
            vmem((NCH, SUB, W, 4 * W), BF16),
            vmem((NCH, SUB, W, 4 * W), BF16),
            vmem((NCH, SUB, W, W), BF16),
            vmem((SUB, W, 2 * W), F32),
            vmem((NCH, SUB, W, W), BF16),
            vmem((NCH, SUB, W, W), BF16),
            vmem((NCH, SUB, W, W), BF16),
            vmem((NCH, SUB, W, W), BF16),
            vmem((NCH, SUB, W, 2 * W), F32),
            dma((NCH, 2)), dma((NCH, 2)),
            dma((NCH, 2, 3)), dma((NCH, 2, 3)),
            dma((NCH, 4, 2)), dma((NCH, 4, 2)),
            dma((NCH,)), dma((NCH,)), dma((NCH, 2)),
            dma((NCH, 2)), dma((NCH, 2)), dma((NCH, 3)), dma((NCH, 2)),
            dma((NCH, 2)), dma((NCH, 2)), dma((NCH, 2)), dma((NCH, 2)),
            dma((NCH,)), dma((NCH,)), dma((NCH,)), dma((NCH,)),
        ],
        compiler_params=pltpu.CompilerParams(
            collective_id=0, has_side_effects=True, vmem_limit_bytes=56 * 2**20
        ),
        cost_estimate=pl.CostEstimate(flops=17179869184, bytes_accessed=2 * 2**20, transcendentals=0),
        name="step",
    )(u, present, surviving)
    arrived = pl.pallas_call(
        deliver_kernel,
        out_shape=jax.ShapeDtypeStruct((64, B, B), BF16),
        in_specs=[vm, sm, sm],
        out_specs=vm,
        scratch_shapes=[vmem((64, B, B), BF16), dma((16,)), dma((16,)), dma],
        compiler_params=pltpu.CompilerParams(
            collective_id=1, has_side_effects=True, vmem_limit_bytes=24 * 2**20
        ),
        name="deliver",
    )(purified, index, valid)
    return arrived.reshape(64, 1, B * B)


def solution(mesh):
    placed = (P("row", "col"), P("row", "col"), P("row", "col"), P("row", "col"))
    return jax.shard_map(
        per_device, mesh=mesh, in_specs=placed, out_specs=P("row", "col", None), check_vma=False
    )
```

time: 542 us -> 177 us (0.33)
  waiting for transfers between devices: 451 us -> 0 us
  Pallas kernels: 0 us -> 173 us
  blocking collectives: 35.3 us -> 0 us
  matrix products: 30.6 us -> 0 us
  between operations: 13.2 us -> 0.03 us
    all_gather x3 -> x0, waiting for transfers between devices: 450 us -> none  [the longest x2 336 us: multiply(): lax.all_gather(left_tile, 'col', axis=1, tiled=True)]
    pallas_call x0 -> x2, Pallas kernels: none -> 173 us  [the longest x1 130 us: per_device(): pl.pallas_call(step_kernel, out_shape=jax.ShapeDtypeStruct((32, B, B), BF...]
    all_to_all x1 -> x0, blocking collectives: 35.3 us -> none  [per_device(): lax.all_to_all(outgoing, 'row', split_axis=0, concat_axis=0, tiled=True)]
    dot_general x2 -> x0, matrix products: 30.6 us -> none  [multiply(): jnp.dot(lax.all_gather(left_tile, 'col', axis=1, tiled=True), gathered, p...]
  transfers between devices with their start and end apart: 3 -> 0, of which waited for: 3 -> 0; matrix products, arithmetic and copies ran while one was open for 0% -> 0% of each run, Pallas kernels for 0% -> 0%
where the time goes in v1:
time: 177 us
  Pallas kernels  173 us (98%)
  local copies, waits for them, and re-layouts  4.27 us (2%)
    pallas_call x1, Pallas kernels, per_device(): pl.pallas_call(step_kernel, out_shape=jax.ShapeDtypeStruct((32, B, B), BF...  130 us
    pallas_call x1, Pallas kernels, per_device(): pl.pallas_call(deliver_kernel, out_shape=jax.ShapeDtypeStruct((64, B, B),...  42.2 us

profile of v1, /device:TPU:1, one launch (start us, length us, event | category | flops | bytes accessed | tf_op | source)
XLA Modules:
  0.0 177.2 jit_solution(16142376518967898408)
XLA Ops:
  0.0 0.8 reshape.16
  0.8 0.2 convert_reduce_fusion.1
  1.0 0.1 convert_reduce_fusion
  1.0 130.5 %step.1.p = bf16[32,128,128]{2,1,0:T(8,128)(2,1)} custom-call(bf16[512,1024]{1,0:T(8,128)(2,1)} %u.1, s32[4,8]{1,0:T(4,128)} %present.1, s32[4,8]{1,0:T(4,128)} %surviving.1), custom_call_target="tpu_custom_call" | custom-call | flops 17179869184 | bytes 2097152 | tf_op jit(solution)/shard_map/step/pallas_call | solution.py:327
  131.5 0.0 copy-start
  131.5 1.2 copy-done
  132.8 42.2 %deliver.1 = bf16[64,128,128]{2,1,0:T(8,128)(2,1)S(1)} custom-call(bf16[32,128,128]{2,1,0:T(8,128)(2,1)S(1)} %copy-done, s32[64]{0:T(128)S(1)} %get-tuple-element.6.index, s32[64]{0:T(128)S(1)} %get-tuple-element.5.valid), custom_call_target="tpu_custom_call" | custom-call | tf_op jit(solution)/shard_map/deliver/pallas_call | solution.py:358
  174.9 2.3 %reshape.17 = bf16[64,1,16384]{2,0,1:T(8,128)(2,1)} reshape(bf16[64,128,128]{2,1,0:T(8,128)(2,1)S(1)} %deliver.1) | data formatting | bytes 4194304 | tf_op jit(solution)/shard_map/reshape | solution.py:369
  (1 shorter events, 0.0 us)
Async XLA Ops:
  131.5 1.2 copy-start

commit v2 on v0

v2 whole, which is shorter than its diff:
```python
import jax
import jax.numpy as jnp
from jax import lax
from jax.experimental import pallas as pl
from jax.experimental.pallas import tpu as pltpu
from jax.sharding import PartitionSpec as P

MESH = pl.DeviceIdType.MESH
B = 128
ROWS = 512
COLS = 1024
NCH = 4
W = COLS // NCH
SUB = ROWS // W
HS = SUB // 2
UNITS = ((0, 0, 256), (1, 0, 256), (2, 0, 256), (3, 0, 128), (3, 128, 128))
NU = len(UNITS)
BW = W // B
ACROSS = ((2, 0), (2, 1), (1, 0), (3, 1), (3, 0), (1, 1), (0, 1), (0, 0))
F32 = jnp.float32
BF16 = jnp.bfloat16


def coords():
    r = lax.axis_index("row")
    c = lax.axis_index("col")
    return (r // 2) % 4, (r // 8) * 2 + c % 2, c // 2, r % 2


def dev(x, y, z, core):
    x = (x + 8) % 4
    y = (y + 8) % 4
    z = (z + 8) % 4
    return ((y // 2) * 8 + x * 2 + core, z * 2 + y % 2)


def cube_up(chunks, upto, met, cube):
    groups = {}
    for j in chunks:
        groups.setdefault(met.get(j, 0), []).append(j)
        met[j] = upto
    for first, js in groups.items():
        cube(list(range(first, upto)), js[0], js[-1] + 1)


def cols(at, width=W):
    return pl.ds(pl.multiple_of(at * W, W), width)


def step_kernel(
    u, present, surviving, index, valid, out,
    own, right, left, fleft, fown, sums, ssend, srecv, csend, crecv, total, blocks, packed, landed,
    s1s, s1r, s2s, s2r, s3s, s3r, ds_, dr, loc, ls, lr, lrs, lrr, fs, fr, frs, frr, xs, xr, cs, cr, as_, ar,
):
    x, y, z, core = coords()
    yl = y % 2
    q = (x + y) % 2
    bar = pltpu.get_barrier_semaphore()
    xp, xm = dev(x + 1, y, z, core), dev(x - 1, y, z, core)
    yp, ym, yy = dev(x, y + 1, z, core), dev(x, y - 1, z, core), dev(x, y + 2, z, core)
    zp, zm = dev(x, y, z + 1, core), dev(x, y, z - 1, core)
    other = dev(x, y, z, 1 - core)
    partner = dev(x, (y // 2) * 2 + 1 - yl, z, core)
    near = [yp, ym, yy, zp, zm]
    near += [dev(x + dx, y, z, (core + dc) % 2) for dx, dc in ACROSS if (dx, dc) != (0, 0)]
    for d in near:
        pl.semaphore_signal(bar, inc=1, device_id=d, device_id_type=MESH)

    def rc(src, dst, ssem, rsem, to):
        return pltpu.make_async_remote_copy(
            src_ref=src, dst_ref=dst, send_sem=ssem, recv_sem=rsem, device_id=to, device_id_type=MESH
        )

    pending = []

    def go(copy):
        copy.start()
        pending.append(copy)

    def piece(n, xs_, ys_, h):
        xs_ = (xs_ + 8) % 4
        ys_ = (ys_ + 8) % 4
        k = core * (NCH // 2) + h * HS
        j, c, w = UNITS[n]
        return right.at[j, pl.ds(k, HS), ys_ // 2, xs_ // 2, :, pl.ds(pl.multiple_of((ys_ % 2) * W + c, B), w)]

    def sieve(j):
        for i in range(4):
            for b in range(BW):
                keep = present[i, j * BW + b] != 0
                block = u[i * B:(i + 1) * B, j * W + b * B:j * W + (b + 1) * B]
                r0 = (i * B) % W
                kept = jnp.where(keep, block, jnp.zeros_like(block))
                own[0, j, (i * B) // W, r0:r0 + B, b * B:(b + 1) * B] = kept

    def part(h):
        return pl.ds(h * HS, HS)

    def shift(h):
        return 1 if h else -1

    def mine(g, n, h):
        j, c, w = UNITS[n]
        return own.at[g, j, part(h), :, pl.ds(c, w)]

    def st1(n):
        for h in range(2):
            go(rc(mine(0, n, h), mine(1, n, h), s1s.at[n, h], s1r.at[n, h], xm if h else xp))

    def along_x(j, h, d, src):
        at = piece(j, x + q * shift(h), y + d, h)
        to = dev(x + shift(h) * (1 - 2 * q), y, z, core)
        go(rc(at if src is None else src, at, s3s.at[j, d % 4, h], s3r.at[j, d % 4, h], to))

    def st1_wait(n):
        for h in range(2):
            rc(mine(0, n, h), mine(1, n, h), s1s.at[n, h], s1r.at[n, h], xp).wait_recv()

    def st2(n):
        for h in range(2):
            wrong = mine(1 - q, n, h)
            fine = mine(q, n, h)
            wx = x + (1 - q) * shift(h)
            fx = x + q * shift(h)
            go(rc(wrong, piece(n, wx, y, h), s2s.at[n, h, 0], s2r.at[n, h, 0], yp))
            go(rc(wrong, piece(n, wx, y, h), s2s.at[n, h, 1], s2r.at[n, h, 1], ym))
            go(rc(fine, piece(n, fx, y, h), s2s.at[n, h, 2], s2r.at[n, h, 2], yy))

    def st2_here(n):
        for h in range(2):
            fine = mine(q, n, h)
            along_x(n, h, 0, fine)
            pltpu.make_async_copy(fine, piece(n, x + q * shift(h), y, h), loc.at[n, h]).start()

    def hand_over(n, xs_, h):
        j, c, w = UNITS[n]
        k = core * (NCH // 2) + h * HS
        for c0, wide in ((0, 2 * W),) if w == W else ((c, w), (W + c, w)):
            at = right.at[j, pl.ds(k, HS), :, ((xs_ + 8) % 4) // 2, :, pl.ds(c0, wide)]
            rc(at, at, ds_.at[n], dr.at[n], other).start()

    def st3(j, kinds):
        for kind in kinds:
            for h in range(2):
                d = (-1, 1, 2)[kind]
                at = piece(j, x + q * shift(h), y + d, h)
                rc(at, at, s2s.at[j, h, kind], s2r.at[j, h, kind], yp).wait_recv()
                along_x(j, h, d, None)

    def share_first(j):
        for h in range(2):
            at = mine(q, j, h)
            pltpu.make_async_copy(at, piece(j, x + q * shift(h), y, h), loc.at[j, h]).wait()
            hand_over(j, x + q * shift(h), h)

    def share(j):
        for h in range(2):
            for d in (0, -1, 1, 2):
                at = piece(j, x + q * shift(h) + 2, y + d, h)
                rc(at, at, s3s.at[j, d % 4, h], s3r.at[j, d % 4, h], xp).wait_recv()
            hand_over(j, x + q * shift(h) + 2, h)

    def half(n, core_):
        j, c, w = UNITS[n]
        k = pl.ds(core_ * (NCH // 2), NCH // 2)
        return right.at[j, k, :, :, :, pl.ds(0, 2 * w)]

    def l_send(j, k):
        return rc(own.at[0, j], left.at[j, :, :, cols(z)], ls.at[j, k], lr.at[j, k], (zp, zm)[k])

    def l_relay(j, k):
        on = left.at[j, part(k), :, cols((z + (3, 1)[k]) % 4)]
        return rc(on, on, lrs.at[j, k], lrr.at[j, k], (zp, zm)[k])

    def f_send(n, m, k):
        j, c, w = UNITS[n]
        at = fleft.at[j, m, :, pl.ds(pl.multiple_of(z * W + c, B), w)]
        return rc(fown.at[j, m, :, pl.ds(c, w)], at, fs.at[n, m, k], fr.at[n, m, k], (zp, zm)[k])

    def f_relay(n, m, k):
        j, c, w = UNITS[n]
        lane = pl.multiple_of(((z + (3, 1)[k]) % 4) * W + c, B)
        on = fleft.at[j, m, pl.ds(k * (W // 2), W // 2), pl.ds(lane, w)]
        return rc(on, on, frs.at[n, m, k], frr.at[n, m, k], (zp, zm)[k])

    def s_send(n, m):
        j, c, w = UNITS[n]
        at = pl.ds(c, w)
        return rc(ssend.at[j, m, :, at], srecv.at[j, m, :, at], xs.at[n, m], xr.at[n, m], partner)

    def c_send(j, m):
        return rc(csend.at[j, m], crecv.at[j, m], cs.at[j, m], cr.at[j, m], partner)

    def own_left(j):
        return pltpu.make_async_copy(own.at[0, j], left.at[j, :, :, cols(z)], ls.at[j, 2])

    def square(n):
        j, c, w = UNITS[n]
        rc(half(n, core), half(n, 1 - core), ds_.at[n], dr.at[n], other).wait_recv()

        @pl.loop(0, SUB)
        def _(m):
            acc = None
            for k in range(NCH):
                if w == W:
                    r = right[j, k].reshape(4 * W, 2 * W)
                else:
                    r = [right[j, k, :, :, :, c0:c0 + w].reshape(4 * W, w) for c0 in (c, W + c)]
                    r = jnp.concatenate(r, axis=1)
                d = jnp.dot(left[k, m], r, preferred_element_type=F32)
                acc = d if acc is None else acc + d
            sums[m, :, 0:2 * w] = acc
            ssend[j, m, :, c:c + w] = sums[m, :, pl.ds(pl.multiple_of((1 - yl) * w, B), w)].astype(BF16)
            s_send(n, m).start()

    def sift(n):
        j, c, w = UNITS[n]

        @pl.loop(0, SUB)
        def _(m):
            s_send(n, m).wait_recv()
            for i in range(W // B):
                rows = slice(i * B, (i + 1) * B)
                for b in range(c // B, (c + w) // B):
                    keep = surviving[m * (W // B) + i, j * BW + b].astype(F32)
                    at = pl.ds(pl.multiple_of(yl * w + b * B - c, B), B)
                    mine_ = pl.ds(pl.multiple_of(yl * W + b * B, B), B)
                    cb = slice(b * B, (b + 1) * B)
                    f = (sums[m, rows, at] + srecv[j, m, rows, cb].astype(F32)) * keep
                    fb = f.astype(BF16)
                    fown[j, m, rows, cb] = fb
                    fleft[j, m, rows, pl.ds(pl.multiple_of(z * W + b * B, B), B)] = fb
                    total[j, m, rows, mine_] = total[j, m, rows, mine_] + f * -1.5
            for k in range(2):
                f_send(n, m, k).start()

    def sift_relay(j):
        @pl.loop(0, SUB)
        def _(m):
            for k in range(2):
                f_send(j, m, k).wait_recv()
                f_relay(j, m, k).start()

    def sift_wait(j):
        @pl.loop(0, SUB)
        def _(m):
            for k in range(2):
                f_relay(j, m, k).wait_recv()

    def cubed(n, j, m):
        k, c, w = UNITS[n]
        if w == W:
            return jnp.dot(fleft[k, m], right[j, k].reshape(4 * W, 2 * W), preferred_element_type=F32)
        f = jnp.concatenate([fleft[k, m, :, i * W + c:i * W + c + w] for i in range(4)], axis=1)
        r = right[j, k, :, :, c:c + w, :].reshape(4 * w, 2 * W)
        return jnp.dot(f, r, preferred_element_type=F32)

    def cube(ns, j0, j1):
        if not len(ns) or j0 >= j1:
            return

        @pl.loop(j0, j1)
        def _(j):
            @pl.loop(0, SUB)
            def _(m):
                acc = total[j, m]
                for n in ns:
                    acc += cubed(n, j, m)
                total[j, m] = acc

    last = NU - 1
    sieve(0)
    pl.semaphore_wait(bar, len(near))
    st1(0)
    for j in range(NCH):
        if j:
            sieve(j)
        own_left(j).start()
        for k in range(2):
            l_send(j, k).start()
    st1(1)

    met = {}
    for t in range(NU + 2):
        s = t - 2
        if 1 <= t <= NU:
            st3(t - 1, (0,))
        if t == 0:
            st1_wait(0)
            st2(0)
            st2_here(0)
            for n in range(2, NU):
                st1(n)
            st1_wait(1)
            st2_here(1)
            total[...] = jnp.zeros_like(total)
        elif t < NU:
            st2(t)
            if t + 1 < NU:
                st1_wait(t + 1)
                st2_here(t + 1)
        if 1 <= t <= NU:
            st3(t - 1, (1, 2))
            share_first(t - 1)
        if s >= 1:
            sift(s - 1)
        if t == 1:
            for j in range(NCH):
                for k in range(2):
                    l_send(j, k).wait_recv()
                    l_relay(j, k).start()
        if s < 0:
            continue
        share(s)
        if s == 0:
            for j in range(NCH):
                own_left(j).wait()
                for k in range(2):
                    l_relay(j, k).wait_recv()
        square(s)
        if s >= 1:
            sift_relay(s - 1)
        if s >= 2:
            sift_wait(s - 2)
            ready = [j for j in range(NCH) if all(n <= s for n in range(NU) if UNITS[n][0] == j)]
            cube_up(ready, s - 1, met, cube)
    sift(last)
    sift_wait(last - 1)
    cube_up(list(range(NCH)), last, met, cube)
    sift_relay(last)

    @pl.loop(0, SUB)
    def _(m):
        for k in range(2):
            f_relay(last, m, k).wait_recv()

        @pl.loop(0, NCH)
        def _(j):
            total[j, m] = total[j, m] + cubed(last, j, m)
            csend[j, m] = total[j, m, :, cols(1 - yl)].astype(BF16)
            c_send(j, m).start()

    for copy in pending:
        copy.wait_send()
    for n in range(NU):
        rc(half(n, core), half(n, 1 - core), ds_.at[n], dr.at[n], other).wait_send()
    for j in range(NCH):
        for k in range(2):
            l_send(j, k).wait_send()
            l_relay(j, k).wait_send()
    for n in range(NU):
        for m in range(SUB):
            s_send(n, m).wait_send()
            for k in range(2):
                f_send(n, m, k).wait_send()
                f_relay(n, m, k).wait_send()

    @pl.loop(0, SUB)
    def _(m):
        @pl.loop(0, NCH)
        def _(j):
            c_send(j, m).wait_recv()
            for i in range(W // B):
                for b in range(BW):
                    mine_ = pl.ds(pl.multiple_of(yl * W + b * B, B), B)
                    rows, cb = slice(i * B, (i + 1) * B), slice(b * B, (b + 1) * B)
                    v = (total[j, m, rows, mine_] + crecv[j, m, rows, cb].astype(F32)) * -2.0
                    blocks[(m * (W // B) + i) * 8 + j * BW + b] = v.astype(BF16)

    r = lax.axis_index("row")

    def slot(s):
        block = blocks[index[s]]
        return jnp.where(valid[s] != 0, block, jnp.zeros_like(block))

    there = dev(x, y + 2, z, core)
    copies = []
    for n, (dx, dc) in enumerate(ACROSS):
        to = dev(x + dx, y + 2, z, (core + dc) % 2)
        at = to[0] * 4
        for k in range(4):
            packed[at + k] = slot(at + k)
        copies.append(rc(packed.at[pl.ds(at, 4)], landed.at[n], as_.at[n], ar.at[n], there))
        copies[-1].start()
    for n, (dx, dc) in enumerate(ACROSS):
        if (dx, dc) == (0, 0):
            continue
        to = dev(x + dx, y, z, (core + dc) % 2)
        at = to[0] * 4
        for k in range(4):
            packed[at + k] = slot(at + k)
        copies.append(rc(packed.at[pl.ds(at, 4)], out.at[pl.ds(r * 4, 4)], as_.at[8 + n], ar.at[8 + n], to))
        copies[-1].start()
    for k in range(4):
        out[r * 4 + k] = slot(r * 4 + k)
    for n, (dx, dc) in enumerate(ACROSS):
        to = dev(x + dx, y, z, (core + dc) % 2)
        copies[n].wait_recv()
        at = out.at[pl.ds(there[0] * 4, 4)]
        if (dx, dc) == (0, 0):
            stay = pltpu.make_async_copy(landed.at[n], at, as_.at[16 + n])
            stay.start()
        else:
            copies.append(rc(landed.at[n], at, as_.at[16 + n], ar.at[16 + n], to))
            copies[-1].start()

    @pl.loop(0, NCH)
    def _(j):
        @pl.loop(0, SUB)
        def _(m):
            c_send(j, m).wait_send()

    stay.wait()
    for n, copy in enumerate(copies):
        copy.wait_send()
        if n >= 8:
            copy.wait_recv()


def slots(owners):
    flat = owners.reshape(-1)
    at = jnp.arange(32, dtype=jnp.int32)
    same = flat[:, None] == flat[None, :]
    slot = jnp.sum((same & (at[None, :] < at[:, None])).astype(jnp.int32), axis=1)
    target = flat * 4 + slot
    hit = target[None, :] == jnp.arange(64, dtype=jnp.int32)[:, None]
    return jnp.sum(jnp.where(hit, at[None, :], 0), axis=1), jnp.sum(hit.astype(jnp.int32), axis=1)


def per_device(u, present, surviving, owners):
    vm = pl.BlockSpec(memory_space=pltpu.VMEM)
    sm = pl.BlockSpec(memory_space=pltpu.SMEM)
    dma = pltpu.SemaphoreType.DMA
    vmem = pltpu.VMEM
    index, valid = slots(owners)
    arrived = pl.pallas_call(
        step_kernel,
        out_shape=jax.ShapeDtypeStruct((64, B, B), BF16),
        in_specs=[vm, sm, sm, sm, sm],
        out_specs=vm,
        scratch_shapes=[
            vmem((2, NCH, SUB, W, W), BF16),
            vmem((NCH, NCH, 2, 2, W, 2 * W), BF16),
            vmem((NCH, SUB, W, 4 * W), BF16),
            vmem((NCH, SUB, W, 4 * W), BF16),
            vmem((NCH, SUB, W, W), BF16),
            vmem((SUB, W, 2 * W), F32),
            vmem((NCH, SUB, W, W), BF16),
            vmem((NCH, SUB, W, W), BF16),
            vmem((NCH, SUB, W, W), BF16),
            vmem((NCH, SUB, W, W), BF16),
            vmem((NCH, SUB, W, 2 * W), F32),
            vmem((32, B, B), BF16),
            vmem((64, B, B), BF16),
            vmem((8, 4, B, B), BF16),
            dma((NU, 2)), dma((NU, 2)),
            dma((NU, 2, 3)), dma((NU, 2, 3)),
            dma((NU, 4, 2)), dma((NU, 4, 2)),
            dma((NU,)), dma((NU,)), dma((NU, 2)),
            dma((NCH, 3)), dma((NCH, 2)), dma((NCH, 2)), dma((NCH, 2)),
            dma((NU, SUB, 2)), dma((NU, SUB, 2)), dma((NU, SUB, 2)), dma((NU, SUB, 2)),
            dma((NU, SUB)), dma((NU, SUB)), dma((NCH, SUB)), dma((NCH, SUB)),
            dma((24,)), dma((24,)),
        ],
        compiler_params=pltpu.CompilerParams(
            collective_id=0, has_side_effects=True, vmem_limit_bytes=46 * 2**20
        ),
        cost_estimate=pl.CostEstimate(flops=17179869184, bytes_accessed=2 * 2**20, transcendentals=0),
        name="step",
    )(u, present, surviving, index, valid)
    return arrived.reshape(64, 1, B * B)


def solution(mesh):
    placed = (P("row", "col"), P("row", "col"), P("row", "col"), P("row", "col"))
    return jax.shard_map(
        per_device, mesh=mesh, in_specs=placed, out_specs=P("row", "col", None), check_vma=False
    )
```

time: 542 us -> 159 us (0.29)
  waiting for transfers between devices: 451 us -> 0 us
  Pallas kernels: 0 us -> 153 us
  blocking collectives: 35.3 us -> 0 us
  matrix products: 30.6 us -> 0 us
  between operations: 13.2 us -> 0.02 us
    all_gather x3 -> x0, waiting for transfers between devices: 450 us -> none  [the longest x2 336 us: multiply(): lax.all_gather(left_tile, 'col', axis=1, tiled=True)]
    pallas_call x0 -> x1, Pallas kernels: none -> 153 us  [per_device(): pl.pallas_call(step_kernel, out_shape=jax.ShapeDtypeStruct((64, B, B), BF...]
    all_to_all x1 -> x0, blocking collectives: 35.3 us -> none  [per_device(): lax.all_to_all(outgoing, 'row', split_axis=0, concat_axis=0, tiled=True)]
    dot_general x2 -> x0, matrix products: 30.6 us -> none  [multiply(): jnp.dot(lax.all_gather(left_tile, 'col', axis=1, tiled=True), gathered, p...]
  transfers between devices with their start and end apart: 3 -> 0, of which waited for: 3 -> 0; matrix products, arithmetic and copies ran while one was open for 0% -> 0% of each run, Pallas kernels for 0% -> 0%
where the time goes in v2:
time: 159 us; the launch traced here: 158 us
  Pallas kernels  153 us (96%)
  local copies, waits for them, and re-layouts  5.64 us (4%)
    pallas_call x1, Pallas kernels, per_device(): pl.pallas_call(step_kernel, out_shape=jax.ShapeDtypeStruct((64, B, B), BF...  153 us

profile of v2, /device:TPU:1, one launch (start us, length us, event | category | flops | bytes accessed | tf_op | source)
XLA Modules:
  0.0 158.5 jit_solution(8338511932210465963)
XLA Ops:
  0.0 0.8 reshape.16
  0.8 0.2 convert_reduce_fusion.1
  1.0 0.1 convert_reduce_fusion
  1.0 0.0 copy-start
  1.1 1.2 copy-done
  2.3 0.0 copy-start.1
  2.3 0.7 copy-done.1
  3.0 0.0 copy-start.2
  3.0 0.7 copy-done.2
  3.6 152.5 %step.1 = bf16[64,128,128]{2,1,0:T(8,128)(2,1)S(1)} custom-call(bf16[512,1024]{1,0:T(8,128)(2,1)S(1)} %copy-done, s32[4,8]{1,0:T(4,128)S(1)} %copy-done.1, s32[4,8]{1,0:T(4,128)S(1)} %copy-done.2, s32[64]{0:T(128)S(1)} %get-tuple-element.6.index, s32[64]{0:T(128)S(1)} %get-tuple-element.5.valid), custom_call_target="tpu_custom_call" | custom-call | flops 17179869184 | bytes 2097152 | tf_op jit(solution)/shard_map/step/pallas_call | solution.py:436
  156.2 2.3 %reshape.17 = bf16[64,1,16384]{2,0,1:T(8,128)(2,1)} reshape(bf16[64,128,128]{2,1,0:T(8,128)(2,1)S(1)} %step.1) | data formatting | bytes 4194304 | tf_op jit(solution)/shard_map/reshape | solution.py:471
  (1 shorter events, 0.0 us)
Async XLA Ops:
  1.0 1.2 copy-start
  2.3 0.7 copy-start.1
  3.0 0.7 copy-start.2

commit v3 on v2

--- a/solution.py
+++ b/solution.py
@@ -15,6 +15,8 @@
 HS = SUB // 2
 UNITS = ((0, 0, 256), (1, 0, 256), (2, 0, 256), (3, 0, 128), (3, 128, 128))
 NU = len(UNITS)
+FLIGHT = 3
+EARLY = 1
 BW = W // B
 ACROSS = ((2, 0), (2, 1), (1, 0), (3, 1), (3, 0), (1, 1), (0, 1), (0, 0))
 F32 = jnp.float32
@@ -48,8 +50,8 @@
 
 
 def step_kernel(
-    u, present, surviving, index, valid, out,
-    own, right, left, fleft, fown, sums, ssend, srecv, csend, crecv, total, blocks, packed, landed,
+    u, present, surviving, owned, out,
+    own, right, left, fleft, fown, sums, ssend, srecv, csend, crecv, total, blocks, packed, landed, index, valid,
     s1s, s1r, s2s, s2r, s3s, s3r, ds_, dr, loc, ls, lr, lrs, lrr, fs, fr, frs, frr, xs, xr, cs, cr, as_, ar,
 ):
     x, y, z, core = coords()
@@ -84,6 +86,25 @@
         j, c, w = UNITS[n]
         return right.at[j, pl.ds(k, HS), ys_ // 2, xs_ // 2, :, pl.ds(pl.multiple_of((ys_ % 2) * W + c, B), w)]
 
+    def number_slots():
+        at = []
+        for b in range(32):
+            o = owned[b // 8, b % 8]
+            rank = jnp.int32(0)
+            for e in range(b):
+                rank += (owned[e // 8, e % 8] == o).astype(jnp.int32)
+            at.append(o * 4 + rank)
+
+        @pl.loop(0, 64)
+        def _(n):
+            which, found = jnp.int32(0), jnp.int32(0)
+            for b in range(32):
+                hit = at[b] == n
+                which = jnp.where(hit, b, which)
+                found = jnp.where(hit, 1, found)
+            index[n] = which
+            valid[n] = found
+
     def sieve(j):
         for i in range(4):
             for b in range(BW):
@@ -165,12 +186,13 @@
         k = pl.ds(core_ * (NCH // 2), NCH // 2)
         return right.at[j, k, :, :, :, pl.ds(0, 2 * w)]
 
-    def l_send(j, k):
-        return rc(own.at[0, j], left.at[j, :, :, cols(z)], ls.at[j, k], lr.at[j, k], (zp, zm)[k])
-
-    def l_relay(j, k):
-        on = left.at[j, part(k), :, cols((z + (3, 1)[k]) % 4)]
-        return rc(on, on, lrs.at[j, k], lrr.at[j, k], (zp, zm)[k])
+    def l_send(m, k):
+        at = left.at[:, m, :, cols(z)]
+        return rc(own.at[0, :, m], at, ls.at[m, k], lr.at[m, k], (zp, zm)[k])
+
+    def l_relay(m, k):
+        on = left.at[:, m, pl.ds(k * (W // 2), W // 2), cols((z + (3, 1)[k]) % 4)]
+        return rc(on, on, lrs.at[m, k], lrr.at[m, k], (zp, zm)[k])
 
     def f_send(n, m, k):
         j, c, w = UNITS[n]
@@ -196,10 +218,12 @@
 
     def square(n):
         j, c, w = UNITS[n]
+        if n == 0:
+            for i in range(NCH):
+                own_left(i).wait()
         rc(half(n, core), half(n, 1 - core), ds_.at[n], dr.at[n], other).wait_recv()
 
-        @pl.loop(0, SUB)
-        def _(m):
+        def rows(m):
             acc = None
             for k in range(NCH):
                 if w == W:
@@ -213,10 +237,18 @@
             ssend[j, m, :, c:c + w] = sums[m, :, pl.ds(pl.multiple_of((1 - yl) * w, B), w)].astype(BF16)
             s_send(n, m).start()
 
-    def sift(n):
-        j, c, w = UNITS[n]
-
-        @pl.loop(0, SUB)
+        if n:
+            pl.loop(0, SUB)(rows)
+        else:
+            for m in range(SUB):
+                for k in range(2):
+                    l_relay(m, k).wait_recv()
+                rows(m)
+
+    def sift(n, m0=0, m1=SUB):
+        j, c, w = UNITS[n]
+
+        @pl.loop(m0, m1)
         def _(m):
             s_send(n, m).wait_recv()
             for i in range(W // B):
@@ -276,13 +308,19 @@
         if j:
             sieve(j)
         own_left(j).start()
-        for k in range(2):
-            l_send(j, k).start()
+    for k in range(2):
+        l_send(0, k).start()
     st1(1)
 
     met = {}
     for t in range(NU + 2):
         s = t - 2
+        if t == 1:
+            for k in range(2):
+                l_send(0, k).wait_recv()
+                l_relay(0, k).start()
+            for k in range(2):
+                l_send(1, k).start()
         if 1 <= t <= NU:
             st3(t - 1, (0,))
         if t == 0:
@@ -303,21 +341,17 @@
             st3(t - 1, (1, 2))
             share_first(t - 1)
         if s >= 1:
-            sift(s - 1)
-        if t == 1:
-            for j in range(NCH):
-                for k in range(2):
-                    l_send(j, k).wait_recv()
-                    l_relay(j, k).start()
+            sift(s - 1, EARLY if s == 1 else 0)
+        if t == 2:
+            for k in range(2):
+                l_send(1, k).wait_recv()
+                l_relay(1, k).start()
         if s < 0:
             continue
         share(s)
-        if s == 0:
-            for j in range(NCH):
-                own_left(j).wait()
-                for k in range(2):
-                    l_relay(j, k).wait_recv()
         square(s)
+        if s == 0 and EARLY:
+            sift(0, 0, 1)
         if s >= 1:
             sift_relay(s - 1)
         if s >= 2:
@@ -340,14 +374,15 @@
             csend[j, m] = total[j, m, :, cols(1 - yl)].astype(BF16)
             c_send(j, m).start()
 
+    number_slots()
     for copy in pending:
         copy.wait_send()
     for n in range(NU):
         rc(half(n, core), half(n, 1 - core), ds_.at[n], dr.at[n], other).wait_send()
-    for j in range(NCH):
+    for m in range(SUB):
         for k in range(2):
-            l_send(j, k).wait_send()
-            l_relay(j, k).wait_send()
+            l_send(m, k).wait_send()
+            l_relay(m, k).wait_send()
     for n in range(NU):
         for m in range(SUB):
             s_send(n, m).wait_send()
@@ -375,13 +410,18 @@
 
     there = dev(x, y + 2, z, core)
     copies = []
-    for n, (dx, dc) in enumerate(ACROSS):
-        to = dev(x + dx, y + 2, z, (core + dc) % 2)
-        at = to[0] * 4
+
+    def over(n):
+        dx, dc = ACROSS[n]
+        at = dev(x + dx, y + 2, z, (core + dc) % 2)[0] * 4
         for k in range(4):
             packed[at + k] = slot(at + k)
         copies.append(rc(packed.at[pl.ds(at, 4)], landed.at[n], as_.at[n], ar.at[n], there))
         copies[-1].start()
+
+    for n in range(FLIGHT):
+        over(n)
+    along = []
     for n, (dx, dc) in enumerate(ACROSS):
         if (dx, dc) == (0, 0):
             continue
@@ -389,20 +429,22 @@
         at = to[0] * 4
         for k in range(4):
             packed[at + k] = slot(at + k)
-        copies.append(rc(packed.at[pl.ds(at, 4)], out.at[pl.ds(r * 4, 4)], as_.at[8 + n], ar.at[8 + n], to))
-        copies[-1].start()
+        along.append(rc(packed.at[pl.ds(at, 4)], out.at[pl.ds(r * 4, 4)], as_.at[8 + n], ar.at[8 + n], to))
+        along[-1].start()
     for k in range(4):
         out[r * 4 + k] = slot(r * 4 + k)
     for n, (dx, dc) in enumerate(ACROSS):
         to = dev(x + dx, y, z, (core + dc) % 2)
         copies[n].wait_recv()
+        if n + FLIGHT < 8:
+            over(n + FLIGHT)
         at = out.at[pl.ds(there[0] * 4, 4)]
         if (dx, dc) == (0, 0):
             stay = pltpu.make_async_copy(landed.at[n], at, as_.at[16 + n])
             stay.start()
         else:
-            copies.append(rc(landed.at[n], at, as_.at[16 + n], ar.at[16 + n], to))
-            copies[-1].start()
+            along.append(rc(landed.at[n], at, as_.at[16 + n], ar.at[16 + n], to))
+            along[-1].start()
 
     @pl.loop(0, NCH)
     def _(j):
@@ -411,20 +453,10 @@
             c_send(j, m).wait_send()
 
     stay.wait()
-    for n, copy in enumerate(copies):
+    for copy in copies:
         copy.wait_send()
-        if n >= 8:
-            copy.wait_recv()
-
-
-def slots(owners):
-    flat = owners.reshape(-1)
-    at = jnp.arange(32, dtype=jnp.int32)
-    same = flat[:, None] == flat[None, :]
-    slot = jnp.sum((same & (at[None, :] < at[:, None])).astype(jnp.int32), axis=1)
-    target = flat * 4 + slot
-    hit = target[None, :] == jnp.arange(64, dtype=jnp.int32)[:, None]
-    return jnp.sum(jnp.where(hit, at[None, :], 0), axis=1), jnp.sum(hit.astype(jnp.int32), axis=1)
+    for copy in along:
+        copy.wait()
 
 
 def per_device(u, present, surviving, owners):
@@ -432,11 +464,10 @@
     sm = pl.BlockSpec(memory_space=pltpu.SMEM)
     dma = pltpu.SemaphoreType.DMA
     vmem = pltpu.VMEM
-    index, valid = slots(owners)
     arrived = pl.pallas_call(
         step_kernel,
         out_shape=jax.ShapeDtypeStruct((64, B, B), BF16),
-        in_specs=[vm, sm, sm, sm, sm],
+        in_specs=[vm, sm, sm, sm],
         out_specs=vm,
         scratch_shapes=[
             vmem((2, NCH, SUB, W, W), BF16),
@@ -453,6 +484,8 @@
             vmem((32, B, B), BF16),
             vmem((64, B, B), BF16),
             vmem((8, 4, B, B), BF16),
+            pltpu.SMEM((64,), jnp.int32),
+            pltpu.SMEM((64,), jnp.int32),
             dma((NU, 2)), dma((NU, 2)),
             dma((NU, 2, 3)), dma((NU, 2, 3)),
             dma((NU, 4, 2)), dma((NU, 4, 2)),
@@ -467,7 +500,7 @@
         ),
         cost_estimate=pl.CostEstimate(flops=17179869184, bytes_accessed=2 * 2**20, transcendentals=0),
         name="step",
-    )(u, present, surviving, index, valid)
+    )(u, present, surviving, owners)
     return arrived.reshape(64, 1, B * B)
 
 

time: 159 us -> 158 us (level)
    unnamed x6 -> x8, local copies, waits for them, and re-layouts: 2.59 us -> 3.27 us
where the time goes in v3:
time: 158 us
  Pallas kernels  152 us (96%)
  local copies, waits for them, and re-layouts  5.56 us (4%)
    pallas_call x1, Pallas kernels, per_device(): pl.pallas_call(step_kernel, out_shape=jax.ShapeDtypeStruct((64, B, B), BF...  152 us
    unnamed x8, local copies, waits for them, and re-layouts  3.27 us

profile of v3, /device:TPU:1, one launch (start us, length us, event | category | flops | bytes accessed | tf_op | source)
XLA Modules:
  0.0 157.9 jit_solution(3480143286371416117)
XLA Ops:
  0.0 0.0 copy-start
  0.0 1.2 copy-done
  1.2 0.0 copy-start.1
  1.2 0.7 copy-done.1
  1.9 0.0 copy-start.2
  1.9 0.7 copy-done.2
  2.6 0.0 copy-start.3
  2.6 0.7 copy-done.3
  3.3 152.3 %step.1 = bf16[64,128,128]{2,1,0:T(8,128)(2,1)S(1)} custom-call(bf16[512,1024]{1,0:T(8,128)(2,1)S(1)} %copy-done, s32[4,8]{1,0:T(4,128)S(1)} %copy-done.1, s32[4,8]{1,0:T(4,128)S(1)} %copy-done.2, s32[4,8]{1,0:T(4,128)S(1)} %copy-done.3), custom_call_target="tpu_custom_call" | custom-call | flops 17179869184 | bytes 2097152 | tf_op jit(solution)/shard_map/step/pallas_call | solution.py:467
  155.6 2.3 %reshape.3 = bf16[64,1,16384]{2,0,1:T(8,128)(2,1)} reshape(bf16[64,128,128]{2,1,0:T(8,128)(2,1)S(1)} %step.1) | data formatting | bytes 4194304 | tf_op jit(solution)/shard_map/reshape | solution.py:504
Async XLA Ops:
  0.0 1.2 copy-start
  1.2 0.7 copy-start.1
  1.9 0.7 copy-start.2
  2.6 0.7 copy-start.3

commit v4 on v3

--- a/solution.py
+++ b/solution.py
@@ -50,7 +50,7 @@
 
 
 def step_kernel(
-    u, present, surviving, owned, out,
+    u, table, out,
     own, right, left, fleft, fown, sums, ssend, srecv, csend, crecv, total, blocks, packed, landed, index, valid,
     s1s, s1r, s2s, s2r, s3s, s3r, ds_, dr, loc, ls, lr, lrs, lrr, fs, fr, frs, frr, xs, xr, cs, cr, as_, ar,
 ):
@@ -88,11 +88,12 @@
 
     def number_slots():
         at = []
+        owned = [table[b // 8, b % 8] >> 2 for b in range(32)]
         for b in range(32):
-            o = owned[b // 8, b % 8]
+            o = owned[b]
             rank = jnp.int32(0)
             for e in range(b):
-                rank += (owned[e // 8, e % 8] == o).astype(jnp.int32)
+                rank += (owned[e] == o).astype(jnp.int32)
             at.append(o * 4 + rank)
 
         @pl.loop(0, 64)
@@ -108,7 +109,7 @@
     def sieve(j):
         for i in range(4):
             for b in range(BW):
-                keep = present[i, j * BW + b] != 0
+                keep = (table[i, j * BW + b] & 1) != 0
                 block = u[i * B:(i + 1) * B, j * W + b * B:j * W + (b + 1) * B]
                 r0 = (i * B) % W
                 kept = jnp.where(keep, block, jnp.zeros_like(block))
@@ -254,7 +255,7 @@
             for i in range(W // B):
                 rows = slice(i * B, (i + 1) * B)
                 for b in range(c // B, (c + w) // B):
-                    keep = surviving[m * (W // B) + i, j * BW + b].astype(F32)
+                    keep = ((table[m * (W // B) + i, j * BW + b] >> 1) & 1).astype(F32)
                     at = pl.ds(pl.multiple_of(yl * w + b * B - c, B), B)
                     mine_ = pl.ds(pl.multiple_of(yl * W + b * B, B), B)
                     cb = slice(b * B, (b + 1) * B)
@@ -467,7 +468,7 @@
     arrived = pl.pallas_call(
         step_kernel,
         out_shape=jax.ShapeDtypeStruct((64, B, B), BF16),
-        in_specs=[vm, sm, sm, sm],
+        in_specs=[vm, sm],
         out_specs=vm,
         scratch_shapes=[
             vmem((2, NCH, SUB, W, W), BF16),
@@ -500,7 +501,7 @@
         ),
         cost_estimate=pl.CostEstimate(flops=17179869184, bytes_accessed=2 * 2**20, transcendentals=0),
         name="step",
-    )(u, present, surviving, owners)
+    )(u, present + 2 * surviving + 4 * owners)
     return arrived.reshape(64, 1, B * B)
 
 

time: 158 us -> 157 us (level)
  local copies, waits for them, and re-layouts: 5.56 us -> 3.52 us
    unnamed x8 -> x2, local copies, waits for them, and re-layouts: 3.27 us -> 1.22 us
where the time goes in v4:
time: 157 us
  Pallas kernels  152 us (97%)
  local copies, waits for them, and re-layouts  3.52 us (2%)
    pallas_call x1, Pallas kernels, per_device(): pl.pallas_call(step_kernel, out_shape=jax.ShapeDtypeStruct((64, B, B), BF...  152 us

profile of v4, /device:TPU:1, one launch (start us, length us, event | category | flops | bytes accessed | tf_op | source)
XLA Modules:
  0.0 156.5 jit_solution(3256717512997532497)
XLA Ops:
  0.0 0.7 multiply_add_fusion.table
  0.7 0.0 copy-start
  0.7 1.2 copy-done
  1.9 152.3 %step.1 = bf16[64,128,128]{2,1,0:T(8,128)(2,1)S(1)} custom-call(bf16[512,1024]{1,0:T(8,128)(2,1)S(1)} %copy-done, s32[4,8]{1,0:T(4,128)S(1)} %multiply_add_fusion.table), custom_call_target="tpu_custom_call" | custom-call | flops 17179869184 | bytes 2097152 | tf_op jit(solution)/shard_map/step/pallas_call | solution.py:468
  154.2 2.3 %reshape.3 = bf16[64,1,16384]{2,0,1:T(8,128)(2,1)} reshape(bf16[64,128,128]{2,1,0:T(8,128)(2,1)S(1)} %step.1) | data formatting | bytes 4194304 | tf_op jit(solution)/shard_map/reshape | solution.py:505
Async XLA Ops:
  0.7 1.2 copy-start
